TPU v7x, 512 devices: a whole 4x4x16 slice. The times are simulated.
512 devices in a mesh: dp: 64 (over x_hi, z, core), tensor: 8 (over y, x_lo).
Axes of the slice: x: 4 (x_hi: 2, x_lo: 2; x = x_hi * 2 + x_lo), y: 4, z: 16, core: 2. Of those that a mesh axis runs over, the one named last changes fastest.
Arguments:
- out_grads: bfloat16 [3, 4, 8192, 8192], P(None, None, 'dp', 'tensor'), may hold values from -8 to 8
- grad_w: bfloat16 [4, 2048, 8192], P(None, 'dp', 'tensor'), may hold values from -122 to 122
- factor_avg: float32 [512, 64, 64], P(('dp', 'tensor')), may hold values from -1 to 1, as said below
- owner_table: int32 [64], replicated, may hold values from 0 to 63, each once
Outputs:
- update: bfloat16 [4, 2048, 8192], P(None, 'dp', 'tensor')
- fresh: float32 [512, 64, 64], P(('dp', 'tensor'))
Inputs may be any that keep to these rules, and one draw needn't show every extreme that they name: `owner_table`: each block index appears once. `factor_avg`: each block is symmetric with a positive diagonal larger than the sum of magnitudes of its row's other entries.
All inputs are finite; a program needn't handle non-finite values. Where the computation divides by a largest or mean magnitude, that divisor is 1e-20 or more.
Results may differ from a plain program's by a relative error of at most 0.0044.
The roundings to bfloat16 on the way count: a program that leaves them out, or rounds other values in their place, can miss the bound.
Values may be sent and summed in bfloat16 or wider, within the bound.
A program may use at most 64 MiB of HBM per device.

v0:
```python
import jax
import jax.numpy as jnp
from jax import lax
from jax.sharding import PartitionSpec as P

STEPS = 8


average_decay = 0.75
damping = 0.003
kl_clip = 0.1


def shards(out_grads, grad_w, factor_avg, owner_table):
    refresh_count, layer_count, tokens_here, columns = out_grads.shape
    capacity, block_size, _ = factor_avg.shape
    row_count = grad_w.shape[1]
    slot_count = owner_table.shape[0]
    per_layer = columns // block_size
    tokens_all = tokens_here * lax.axis_size("dp")
    weights = [
        (1.0 - average_decay) * average_decay ** (refresh_count - 1 - turn) / tokens_all
        for turn in range(refresh_count)
    ]
    split_grads = out_grads.reshape(refresh_count, layer_count, tokens_here, per_layer, block_size)
    chosen = owner_table
    picked = split_grads[:, chosen // per_layer, :, chosen % per_layer, :]
    summed = jnp.zeros((capacity * lax.axis_size("dp"), block_size, block_size), jnp.float32)
    for turn in range(refresh_count):
        portion = picked[:, turn]
        summed = summed + weights[turn] * jnp.einsum(
            "qtb,qtc->qbc", portion, portion, preferred_element_type=jnp.float32
        )
    grams = lax.psum_scatter(summed, "dp", scatter_dimension=0, tiled=True)
    fresh = average_decay**refresh_count * factor_avg + grams
    identity = jnp.eye(block_size, dtype=jnp.float32)
    damped = fresh + damping * identity
    scale = 1.0 / jnp.max(jnp.sum(jnp.abs(damped), axis=2), axis=1)
    inverse = scale[:, None, None] * identity
    for _ in range(STEPS):
        product = jnp.einsum("qij,qjk->qik", damped, inverse, precision=lax.Precision.HIGHEST)
        inverse = jnp.einsum(
            "qij,qjk->qik", inverse, 2.0 * identity - product, precision=lax.Precision.HIGHEST
        )
    inverse_half = inverse.astype(jnp.bfloat16)
    grad_blocks = grad_w.reshape(layer_count, row_count, per_layer, block_size).transpose(
        0, 2, 1, 3
    )
    grad_blocks = grad_blocks.reshape(slot_count, row_count, block_size)
    slot_of = jnp.argsort(owner_table)
    chosen = owner_table
    ordered_slots = jnp.einsum(
        "qrb,qbc->qrc",
        grad_blocks[chosen],
        lax.all_gather(inverse_half, "dp", axis=0, tiled=True),
        preferred_element_type=jnp.float32,
    ).astype(jnp.bfloat16)
    by_block = ordered_slots[slot_of]
    precond = by_block.reshape(layer_count, per_layer, row_count, block_size).transpose(0, 2, 1, 3)
    precond = precond.reshape(layer_count, row_count, columns)
    local_inner = jnp.sum(grad_w.astype(jnp.float32) * precond.astype(jnp.float32))
    inner = lax.psum(local_inner, ("dp", "tensor"))
    entries = float(
        layer_count * row_count * lax.axis_size("dp") * columns * lax.axis_size("tensor")
    )
    clip = jnp.minimum(1.0, jnp.sqrt(kl_clip * entries / inner))
    update = (clip * precond.astype(jnp.float32)).astype(jnp.bfloat16)
    return (update, fresh)


def solution(mesh):
    placed = (
        P(None, None, "dp", "tensor"),
        P(None, "dp", "tensor"),
        P(("dp", "tensor"), None, None),
        P(),
    )
    return jax.shard_map(
        shards,
        mesh=mesh,
        in_specs=placed,
        out_specs=(P(None, "dp", "tensor"), P(("dp", "tensor"), None, None)),
        check_vma=False,
    )
```

profile of v0, /device:TPU:1, one launch (start us, length us, event | category | flops | bytes accessed | tf_op | source)
XLA Modules:
  0.0 432.8 jit_solution(3581083960140953775)
XLA Ops:
  7.2 0.7 fusion.19
  7.9 4.7 %copy.13 = bf16[3,4,128,1024]{2,3,1,0:T(8,128)(2,1)} copy(bf16[3,4,128,1024]{3,2,1,0:T(8,128)(2,1)} %param.4) | data formatting | bytes 6291456 | tf_op args[0]
  12.6 3.0 gather_fusion.1
  15.6 0.7 fusion
  16.3 0.7 fusion.1
  17.0 2.1 multiply_add_fusion
  19.1 0.9 copy-done.1
  20.0 0.3 reshape.125
  20.5 2.0 sort.17
  22.5 0.7 gather_fusion
  23.2 204.7 %reduce-scatter.2.cloned.1.call-done = f32[1,64,64]{2,1,0:T(8,128)} async-done(((f32[64,64,64]{2,1,0:T(8,128)}), f32[1,64,64]{2,1,0:T(8,128)}) %reduce-scatter.2.cloned.1.call-update) | async-done | bytes 16400 | tf_op jit(solution)/shard_map/reduce_scatter | solution.py:34
  227.9 0.9 abs_reduce_fusion
  228.8 0.6 reduce_max.9
  230.1 0.2 convolution_subtract_fusion.7
  230.4 0.2 convolution_subtract_fusion.6
  230.6 0.2 fusion.24
  230.7 0.2 convolution_subtract_fusion.5
  231.1 0.2 convolution_subtract_fusion.4
  231.3 0.2 fusion.26
  231.4 0.2 convolution_subtract_fusion.3
  231.8 0.2 convolution_subtract_fusion.2
  232.1 0.2 convolution_subtract_fusion.1
  232.4 0.2 convolution_subtract_fusion
  232.6 0.2 convolution_convert_fusion.1
  232.8 88.1 %all-gather = bf16[4096,64]{1,0:T(8,128)(2,1)S(1)} all-gather(bf16[64,64]{1,0:T(8,128)(2,1)S(1)} %convolution_convert_fusion.1), channel_id=2, replica_groups=mesh['dp'=64,'tensor'=8] {'dp'}, dimensions={0}, use_global_device_ids=true | all-gather | bytes 532480 | tf_op jit(solution)/shard_map/all_gather | solution.py:55
  320.9 0.4 convolution_convert_fusion
  321.3 0.7 gather_fusion.2
  322.0 0.6 copy.17
  322.7 0.3 reshape.129
  323.0 0.7 multiply_reduce_fusion
  323.7 100.7 %psum.7 = f32[]{:T(128)} all-reduce(f32[]{:T(128)} %multiply_reduce_fusion), channel_id=1, replica_groups=mesh['dp'=64,'tensor'=8] {'dp','tensor'}, use_global_device_ids=true, to_apply=%region_5.6 | all-reduce | flops 1 | bytes 8 | tf_op jit(solution)/shard_map/psum | solution.py:62
  425.2 0.7 multiply_convert_fusion
  (20 shorter events, 1.2 us)
Async XLA Ops:
  7.2 220.7 %reduce-scatter.2.cloned.1.call-start = ((), (), s32[]{:S(2)}) async-start(), calls=%async_computation.1 | async-start | bytes 2129920 | tf_op jit(solution)/shard_map/reduce_scatter | solution.py:34
  19.0 0.9 copy-start.1
  19.0 1.5 copy-start.3
  19.0 208.9 %copy-start.2 = (f32[1,64,64]{2,1,0:T(8,128)S(1)}, f32[1,64,64]{2,1,0:T(8,128)}, u32[]{:S(2)}) copy-start(f32[1,64,64]{2,1,0:T(8,128)} %param.6) | copy-start | bytes 49156
  228.8 92.5 %copy-start = (f32[1,64,64]{2,1,0:T(8,128)}, f32[1,64,64]{2,1,0:T(8,128)S(1)}, u32[]{:S(2)}) copy-start(f32[1,64,64]{2,1,0:T(8,128)S(1)} %get-tuple-element.5) | copy-start | bytes 49156
Sparse Core Ops, SparseCore 0:
  19.2 208.6 reduce-scatter.1
where the time goes:
time: 433 us
  waiting for transfers between devices  205 us (47%)
  blocking collectives  189 us (44%)
  between operations  15.7 us (4%)
  local copies, waits for them, and re-layouts  11.4 us (3%)
  matrix products  6.38 us (1%)
  other arithmetic  5.8 us (1%)
    reduce_scatter x1, waiting for transfers between devices, shards(): grams = lax.psum_scatter(summed, 'dp', scatter_dimension=0, tiled=True)  205 us
    psum x1, blocking collectives, shards(): inner = lax.psum(local_inner, ('dp', 'tensor'))  101 us
    all_gather x1, blocking collectives, shards(): lax.all_gather(inverse_half, 'dp', axis=0, tiled=True)  88.1 us
  transfers between devices with their start and end apart: 1, of which 1 were waited for; matrix products, arithmetic and copies ran while one was open for 1% of the time, Pallas kernels for 0%

commit v1 on v0

v1 whole, which is shorter than its diff:
```python
import functools

import jax
import jax.numpy as jnp
from jax import lax
from jax.experimental import pallas as pl
from jax.experimental.pallas import tpu as pltpu
from jax.sharding import PartitionSpec as P

STEPS = 8
AVERAGE_DECAY = 0.75
DAMPING = 0.003
KL_CLIP = 0.1
MESH = pl.DeviceIdType.MESH
F32 = jnp.float32
BF16 = jnp.bfloat16


def newton_schulz(damped):
    size = damped.shape[0]
    rows = lax.broadcasted_iota(jnp.int32, (size, size), 0)
    cols = lax.broadcasted_iota(jnp.int32, (size, size), 1)
    identity = jnp.where(rows == cols, 1.0, 0.0).astype(F32)
    scale = 1.0 / jnp.max(jnp.sum(jnp.abs(damped), axis=1, keepdims=True), axis=0, keepdims=True)
    error = identity - scale * damped
    inverse = scale * (identity + error)
    error = jnp.dot(error, error, precision=lax.Precision.HIGHEST, preferred_element_type=F32)
    for step in range(1, STEPS):
        if step < STEPS - 1:
            both = jnp.concatenate([error, inverse], axis=1)
            both = jnp.dot(error, both, precision=lax.Precision.HIGHEST, preferred_element_type=F32)
            inverse = inverse + both[:, size:]
            error = both[:, :size]
        else:
            inverse = inverse + jnp.dot(
                error, inverse, precision=lax.Precision.HIGHEST, preferred_element_type=F32
            )
    return inverse


def exchange_kernel(
    nz, nt, entries, table, og, gw, fa, pre_o, clip_o, fresh_o,
    ybuf, gbuf, fbuf, gram, gblk, mine, snd1, rcv1, snd2, rcv2, xs, xall, inn, tin, xin, cin,
    lsem, s1s, s1r, s2s, s2r, ags, agr, fws, ts, tr, xss, xsr, cs,
):
    refresh, layers, tokens, columns = ybuf.shape
    slots, half, _ = gram.shape
    size = 2 * half
    per_layer = columns // size
    chips = slots // 2
    dp = lax.axis_index("dp")
    t = lax.axis_index("tensor")
    core = lax.rem(dp, 2)
    me = lax.div(dp, 2)
    xh = lax.div(me, nz)
    z = lax.rem(me, nz)
    mate = (dp + 1 - 2 * core, t)

    def far(i):
        j = lax.div(i, 2)
        a = 1 - lax.rem(i, 2)
        k = nz // 2 + lax.div(j + 1, 2) * (1 - 2 * lax.rem(j, 2))
        return lax.rem(xh + a, 2) * nz + lax.rem(z + k, nz)

    others = chips - 1

    def loads():
        out = []
        for l in range(layers):
            for i in range(refresh):
                out.append(pltpu.make_async_copy(og.at[i, l], ybuf.at[i, l], lsem.at[l * refresh + i]))
        return out

    ycopies = loads()
    gcopy = pltpu.make_async_copy(gw, gbuf, lsem.at[layers * refresh])
    fcopy = pltpu.make_async_copy(fa, fbuf, lsem.at[layers * refresh + 1])
    for cp in ycopies[:refresh]:
        cp.start()

    barrier = pltpu.get_barrier_semaphore()

    def greet(i, carry):
        pl.semaphore_signal(barrier, inc=1, device_id=(far(i) * 2 + core, t), device_id_type=MESH)
        return carry

    lax.fori_loop(0, others, greet, 0)
    pl.semaphore_signal(barrier, inc=1, device_id=mate, device_id_type=MESH)
    for k in range(1, nt):
        pl.semaphore_signal(
            barrier, inc=1, device_id=(dp, lax.rem(t + k, nt)), device_id_type=MESH
        )
    for cp in ycopies[refresh:]:
        cp.start()
    gcopy.start()
    fcopy.start()

    weights = [
        (1.0 - AVERAGE_DECAY) * AVERAGE_DECAY ** (refresh - 1 - i) / entries[0] for i in range(refresh)
    ]
    for l in range(layers):
        for i in range(refresh):
            ycopies[l * refresh + i].wait()
        for p in range(per_layer // 2):
            total = None
            for i in range(refresh):
                y = ybuf[i, l, :, 2 * size * p : 2 * size * (p + 1)]
                part = weights[i] * lax.dot_general(
                    y, y, (((0,), (0,)), ((), ())), preferred_element_type=F32
                )
                total = part if total is None else total + part
            b = l * per_layer + 2 * p
            gram[b] = jnp.concatenate([total[:half, :size], total[half:size, :size]], axis=1)
            gram[b + 1] = jnp.concatenate(
                [total[size : size + half, size:], total[size + half :, size:]], axis=1
            )

    def order(q, carry):
        mine[q] = gram[table[2 * q + core]]
        snd1[q] = gram[table[2 * q + 1 - core]].astype(BF16)
        return carry

    lax.fori_loop(0, chips, order, 0)

    gcopy.wait()
    for l in range(layers):
        for j in range(per_layer):
            gblk[l * per_layer + j] = gbuf[l, :, size * j : size * (j + 1)]

    pl.semaphore_wait(barrier, others + nt)

    cp1 = pltpu.make_async_remote_copy(
        src_ref=snd1, dst_ref=rcv1, send_sem=s1s, recv_sem=s1r, device_id=mate, device_id_type=MESH
    )
    cp1.start()
    cp1.wait_recv()

    def scatter(q, slot):
        return pltpu.make_async_remote_copy(
            src_ref=snd2.at[q], dst_ref=rcv2.at[slot], send_sem=s2s.at[q], recv_sem=s2r.at[slot],
            device_id=(q * 2 + core, t), device_id_type=MESH,
        )

    def send_sums(i, carry):
        q = far(i)
        snd2[q] = (mine[q] + rcv1[q].astype(F32)).astype(BF16)
        scatter(q, me).start()
        return carry

    lax.fori_loop(0, others, send_sums, 0)

    def take_sums(i, acc):
        q = far(others - 1 - i)
        scatter(q, q).wait_recv()
        return acc + rcv2[q].astype(F32)

    grams = lax.fori_loop(0, others, take_sums, mine[me] + rcv1[me].astype(F32))
    grams = jnp.concatenate([grams[:, :size], grams[:, size:]], axis=0)
    fcopy.wait()
    fresh = AVERAGE_DECAY**refresh * fbuf[0] + grams
    fresh_o[0] = fresh
    rows = lax.broadcasted_iota(jnp.int32, (size, size), 0)
    cols = lax.broadcasted_iota(jnp.int32, (size, size), 1)
    inverse = newton_schulz(fresh + jnp.where(rows == cols, DAMPING, 0.0))
    packed = jnp.concatenate([inverse[:half], inverse[half:]], axis=1).astype(BF16)
    xs[...] = packed
    xall[core, me] = packed

    def gather(q, slot):
        return pltpu.make_async_remote_copy(
            src_ref=xs, dst_ref=xall.at[core, slot], send_sem=ags.at[q], recv_sem=agr.at[core, slot],
            device_id=(q * 2 + core, t), device_id_type=MESH,
        )

    def forward(q, owner):
        return pltpu.make_async_remote_copy(
            src_ref=xall.at[core, q], dst_ref=xall.at[owner, q], send_sem=fws.at[q],
            recv_sem=agr.at[owner, q], device_id=mate, device_id_type=MESH,
        )

    def send_inverse(i, carry):
        gather(far(i), me).start()
        return carry

    lax.fori_loop(0, others, send_inverse, 0)
    forward(me, core).start()

    def apply(owner, q, acc):
        x = xall[owner, q]
        top, bottom = x[:, :size], x[:, size:]
        x2 = jnp.concatenate(
            [jnp.concatenate([top, top], axis=1), jnp.concatenate([bottom, bottom], axis=1)], axis=0
        )
        g = gblk[table[2 * q + owner]]
        out = jnp.dot(g, x2, preferred_element_type=F32).astype(BF16)
        pre_o[2 * q + owner] = out
        return acc + g.astype(F32) * out[:, :size].astype(F32)

    def take_direct(i, acc):
        q = far(others - 1 - i)
        gather(q, q).wait_recv()
        forward(q, core).start()
        return apply(core, q, acc)

    acc = apply(core, me, jnp.zeros((gbuf.shape[1], size), F32))
    acc = lax.fori_loop(0, others, take_direct, acc)

    def take_forwarded(q, acc):
        forward(q, 1 - core).wait_recv()
        return apply(1 - core, q, acc)

    acc = lax.fori_loop(0, chips, take_forwarded, acc)

    local = jnp.sum(acc, axis=0, keepdims=True)
    local = jnp.concatenate([local, jnp.zeros_like(local)], axis=1)
    inn[0] = local
    tcopies = []
    for k in range(1, nt):
        cp = pltpu.make_async_remote_copy(
            src_ref=inn.at[0], dst_ref=tin.at[k], send_sem=ts.at[k], recv_sem=tr.at[k],
            device_id=(dp, lax.rem(t + k, nt)), device_id_type=MESH,
        )
        cp.start()
        tcopies.append(cp)
    total = local
    for k in range(1, nt):
        tcopies[k - 1].wait_recv()
        total = total + tin[k]
    inn[1] = total

    def spread(q, slot):
        return pltpu.make_async_remote_copy(
            src_ref=inn.at[1], dst_ref=xin.at[slot], send_sem=xss.at[q], recv_sem=xsr.at[slot],
            device_id=(q * 2 + core, t), device_id_type=MESH,
        )

    def send_inner(i, carry):
        spread(far(i), me).start()
        return carry

    lax.fori_loop(0, others, send_inner, 0)

    def take_inner(i, acc):
        q = far(others - 1 - i)
        spread(q, q).wait_recv()
        return acc + xin[q]

    total = lax.fori_loop(0, others, take_inner, total)
    inn[2] = total
    ccopy = pltpu.make_async_remote_copy(
        src_ref=inn.at[2], dst_ref=cin, send_sem=cs.at[0], recv_sem=cs.at[1],
        device_id=mate, device_id_type=MESH,
    )
    ccopy.start()
    ccopy.wait_recv()
    inner = jnp.sum(total + cin[...], axis=1, keepdims=True)
    clip = jnp.minimum(1.0, jnp.sqrt(KL_CLIP * entries[1] / inner))
    clip_o[...] = jnp.broadcast_to(clip, clip_o.shape)

    cp1.wait_send()
    ccopy.wait_send()
    for cp in tcopies:
        cp.wait_send()

    def drain(i, carry):
        q = far(i)
        scatter(q, me).wait_send()
        gather(q, me).wait_send()
        spread(q, me).wait_send()
        forward(q, core).wait_send()
        return carry

    lax.fori_loop(0, others, drain, 0)
    forward(me, core).wait_send()


def finish_kernel(table, pre, clip, fresh, update, fresh_o, slot_of):
    layers, rows, columns = update.shape
    slots = pre.shape[0]
    width = pre.shape[2]
    pairs = columns // width
    fresh_o[...] = fresh[...]

    def invert(r, carry):
        slot_of[table[r]] = r
        return carry

    lax.fori_loop(0, slots, invert, 0)
    factor = clip[0:1, :]
    left = lax.broadcasted_iota(jnp.int32, (rows, width), 1) < width // 2
    for l in range(layers):
        for p in range(pairs):
            b = (l * pairs + p) * 2
            both = jnp.where(left, pre[slot_of[b]].astype(F32), pre[slot_of[b + 1]].astype(F32))
            update[l, :, p * width : (p + 1) * width] = (factor * both).astype(BF16)


def shards(out_grads, grad_w, factor_avg, owner_table):
    refresh, layers, tokens, columns = out_grads.shape
    _, size, _ = factor_avg.shape
    rows = grad_w.shape[1]
    slots = owner_table.shape[0]
    half = size // 2
    n_dp = lax.axis_size("dp")
    nt = lax.axis_size("tensor")
    nz = n_dp // 4
    chips = slots // 2
    entries = (float(tokens * n_dp), float(layers * rows * n_dp * columns * nt))
    dma = pltpu.SemaphoreType.DMA
    hbm = pl.BlockSpec(memory_space=pltpu.HBM)
    vmem = pl.BlockSpec(memory_space=pltpu.VMEM)
    smem = pl.BlockSpec(memory_space=pltpu.SMEM)
    pre, clip, fresh = pl.pallas_call(
        functools.partial(exchange_kernel, nz, nt, entries),
        out_shape=(
            jax.ShapeDtypeStruct((slots, rows, 2 * size), BF16),
            jax.ShapeDtypeStruct((8, 2 * size), F32),
            jax.ShapeDtypeStruct(factor_avg.shape, F32),
        ),
        in_specs=[smem, hbm, hbm, hbm],
        out_specs=(vmem, vmem, vmem),
        scratch_shapes=[
            pltpu.VMEM(out_grads.shape, BF16),
            pltpu.VMEM(grad_w.shape, BF16),
            pltpu.VMEM(factor_avg.shape, F32),
            pltpu.VMEM((slots, half, 2 * size), F32),
            pltpu.VMEM((slots, rows, size), BF16),
            pltpu.VMEM((chips, half, 2 * size), F32),
            pltpu.VMEM((chips, half, 2 * size), BF16),
            pltpu.VMEM((chips, half, 2 * size), BF16),
            pltpu.VMEM((chips, half, 2 * size), BF16),
            pltpu.VMEM((chips, half, 2 * size), BF16),
            pltpu.VMEM((half, 2 * size), BF16),
            pltpu.VMEM((2, chips, half, 2 * size), BF16),
            pltpu.VMEM((3, 1, 2 * size), F32),
            pltpu.VMEM((nt, 1, 2 * size), F32),
            pltpu.VMEM((chips, 1, 2 * size), F32),
            pltpu.VMEM((1, 2 * size), F32),
            dma((layers * refresh + 2,)),
            dma,
            dma,
            dma((chips,)),
            dma((chips,)),
            dma((chips,)),
            dma((2, chips)),
            dma((chips,)),
            dma((nt,)),
            dma((nt,)),
            dma((chips,)),
            dma((chips,)),
            dma((2,)),
        ],
        compiler_params=pltpu.CompilerParams(
            collective_id=0, has_side_effects=True, vmem_limit_bytes=48 * 2**20
        ),
        name="exchange",
    )(owner_table, out_grads, grad_w, factor_avg)
    return pl.pallas_call(
        finish_kernel,
        out_shape=(
            jax.ShapeDtypeStruct(grad_w.shape, BF16),
            jax.ShapeDtypeStruct(factor_avg.shape, F32),
        ),
        in_specs=[smem, vmem, vmem, vmem],
        out_specs=(vmem, vmem),
        scratch_shapes=[pltpu.SMEM((slots,), jnp.int32)],
        compiler_params=pltpu.CompilerParams(vmem_limit_bytes=16 * 2**20),
        name="finish",
    )(owner_table, pre, clip, fresh)


def solution(mesh):
    placed = (
        P(None, None, "dp", "tensor"),
        P(None, "dp", "tensor"),
        P(("dp", "tensor"), None, None),
        P(),
    )
    return jax.shard_map(
        shards,
        mesh=mesh,
        in_specs=placed,
        out_specs=(P(None, "dp", "tensor"), P(("dp", "tensor"), None, None)),
        check_vma=False,
    )
```

time: 433 us -> 87.5 us (0.20)
  waiting for transfers between devices: 205 us -> 0 us
  blocking collectives: 189 us -> 0 us
  Pallas kernels: 0 us -> 82.4 us
  between operations: 15.7 us -> 0.65 us
  local copies, waits for them, and re-layouts: 11.4 us -> 4.24 us
  matrix products: 6.38 us -> 0 us
  other arithmetic: 5.8 us -> 0 us
    reduce_scatter x1 -> x0, waiting for transfers between devices: 205 us -> none  [shards(): grams = lax.psum_scatter(summed, 'dp', scatter_dimension=0, tiled=True)]
    psum x1 -> x0, blocking collectives: 101 us -> none  [shards(): inner = lax.psum(local_inner, ('dp', 'tensor'))]
    all_gather x1 -> x0, blocking collectives: 88.1 us -> none  [shards(): lax.all_gather(inverse_half, 'dp', axis=0, tiled=True)]
    pallas_call x0 -> x2, Pallas kernels: none -> 82.4 us  [the longest x1 80.4 us: shards(): pl.pallas_call(functools.partial(exchange_kernel, nz, nt, entries), out_s...]
    dot_general x20 -> x0, matrix products: 6.38 us -> none  [the longest x3 3.4 us: shards(): jnp.einsum('qtb,qtc->qbc', portion, portion, preferred_element_type=jnp.f...]
    gather x3 -> x0, local copies, waits for them, and re-layouts: 4.35 us -> none  [the longest x1 3.04 us: shards(): picked = split_grads[:, chosen // per_layer, :, chosen % per_layer, :]]
  transfers between devices with their start and end apart: 1 -> 0, of which waited for: 1 -> 0; matrix products, arithmetic and copies ran while one was open for 1% -> 0% of each run, Pallas kernels for 0% -> 0%
where the time goes in v1:
time: 87.5 us; the launch traced here: 87.3 us
  Pallas kernels  82.4 us (94%)
  local copies, waits for them, and re-layouts  4.24 us (5%)
    pallas_call x1, Pallas kernels, shards(): pl.pallas_call(functools.partial(exchange_kernel, nz, nt, entries), out_s...  80.4 us
    unnamed x8, local copies, waits for them, and re-layouts  4.24 us
    pallas_call x1, Pallas kernels, shards(): pl.pallas_call(finish_kernel, out_shape=(jax.ShapeDtypeStruct(grad_w.shap...  1.94 us

profile of v1, /device:TPU:1, one launch (start us, length us, event | category | flops | bytes accessed | tf_op | source)
XLA Modules:
  0.0 87.3 jit_solution(17530755341872082490)
XLA Ops:
  0.6 0.0 copy-start
  0.6 1.9 %copy-done = bf16[3,4,128,1024]{3,2,1,0:T(8,128)(2,1)S(1)} copy-done((bf16[3,4,128,1024]{3,2,1,0:T(8,128)(2,1)S(1)}, bf16[3,4,128,1024]{3,2,1,0:T(8,128)(2,1)}, u32[]{:S(2)}) %copy-start) | copy-done | bytes 3145752
  2.5 0.0 copy-start.1
  2.5 0.9 %copy-done.1 = bf16[4,32,1024]{2,1,0:T(8,128)(2,1)S(1)} copy-done((bf16[4,32,1024]{2,1,0:T(8,128)(2,1)S(1)}, bf16[4,32,1024]{2,1,0:T(8,128)(2,1)}, u32[]{:S(2)}) %copy-start.1) | copy-done | bytes 262168
  3.5 0.0 copy-start.2
  3.5 0.8 copy-done.2
  4.2 0.0 copy-start.3
  4.2 0.7 copy-done.3
  4.9 80.4 %exchange.1 = (bf16[64,32,128]{2,1,0:T(8,128)(2,1)S(1)}, f32[8,128]{1,0:T(8,128)S(1)}, f32[1,64,64]{2,1,0:T(8,128)S(1)}) custom-call(s32[64]{0:T(128)S(1)} %copy-done.3, bf16[3,4,128,1024]{3,2,1,0:T(8,128)(2,1)S(1)} %copy-done, bf16[4,32,1024]{2,1,0:T(8,128)(2,1)S(1)} %copy-done.1, f32[1,64,64]{2,1,0:T(8,128)S(1)} %copy-done.2), custom_call_target="tpu_custom_call" | custom-call | tf_op jit(solution)/shard_map/exchange/pallas_call | solution.py:312
  85.3 1.9 %finish.1 = (bf16[4,32,1024]{2,1,0:T(8,128)(2,1)}, f32[1,64,64]{2,1,0:T(8,128)}) custom-call(s32[64]{0:T(128)S(1)} %copy-done.3, bf16[64,32,128]{2,1,0:T(8,128)(2,1)S(1)} %get-tuple-element.5.pre, f32[8,128]{1,0:T(8,128)S(1)} %get-tuple-element.6.clip, f32[1,64,64]{2,1,0:T(8,128)S(1)} %get-tuple-element.7.fresh), custom_call_target="tpu_custom_call" | custom-call | tf_op jit(solution)/shard_map/finish/pallas_call | solution.py:357
Async XLA Ops:
  0.6 1.9 %copy-start = (bf16[3,4,128,1024]{3,2,1,0:T(8,128)(2,1)S(1)}, bf16[3,4,128,1024]{3,2,1,0:T(8,128)(2,1)}, u32[]{:S(2)}) copy-start(bf16[3,4,128,1024]{3,2,1,0:T(8,128)(2,1)} %og.1) | copy-start | bytes 9437188
  2.5 0.9 %copy-start.1 = (bf16[4,32,1024]{2,1,0:T(8,128)(2,1)S(1)}, bf16[4,32,1024]{2,1,0:T(8,128)(2,1)}, u32[]{:S(2)}) copy-start(bf16[4,32,1024]{2,1,0:T(8,128)(2,1)} %gw.1) | copy-start | bytes 786436
  3.5 0.8 copy-start.2
  4.2 0.7 copy-start.3

commit v2 on v0

v2 whole, which is shorter than its diff:
```python
import functools

import jax
import jax.numpy as jnp
from jax import lax
from jax.experimental import pallas as pl
from jax.experimental.pallas import tpu as pltpu
from jax.sharding import PartitionSpec as P

STEPS = 8
AVERAGE_DECAY = 0.75
DAMPING = 0.003
KL_CLIP = 0.1
MESH = pl.DeviceIdType.MESH
F32 = jnp.float32
BF16 = jnp.bfloat16


def iota(shape, axis):
    return lax.broadcasted_iota(jnp.int32, shape, axis)


def newton_schulz(damped):
    size = damped.shape[0]
    identity = jnp.where(iota((size, size), 0) == iota((size, size), 1), 1.0, 0.0).astype(F32)

    def dot(a, b):
        return jnp.dot(a, b, precision=lax.Precision.HIGHEST, preferred_element_type=F32)

    scale = 1.0 / jnp.max(jnp.sum(jnp.abs(damped), axis=1, keepdims=True), axis=0, keepdims=True)
    error = identity - scale * damped
    inverse = scale * (identity + error)
    for _ in range(1, STEPS):
        error = dot(error, error)
        inverse = inverse + dot(error, inverse)
    return inverse


def pack_pair(total, body, diag, b):
    wide = total.shape[0]
    size, half, quarter = wide // 2, wide // 4, wide // 8
    row, lane = iota((half, wide), 0), iota((half, wide), 1)
    first = lane < size
    local = jnp.where(first, lane, lane - size)
    upper = jnp.where(first, total[:half], total[size : size + half])
    lower = jnp.where(first, total[half:size], total[size + half :])
    moved = pltpu.roll(lower, wide - half, 1)
    both = jnp.where((local < half) & (row > local), moved, upper)
    turned = pltpu.roll(both, size, 1)
    side = iota((quarter, wide), 1) < size
    body[b] = jnp.where(side, both[:quarter], turned[quarter:])
    body[b + 1] = jnp.where(side, turned[:quarter], both[quarter:])
    on = jnp.where(row == local, upper, 0.0) + jnp.where(row + half == local, lower, 0.0)
    on = jnp.sum(on, axis=0, keepdims=True)
    swapped = pltpu.roll(on, size, 1)
    side = iota((1, wide), 1) < size
    diag[b] = jnp.where(side, on, swapped)
    diag[b + 1] = jnp.where(side, swapped, on)


def unpack(body, diag):
    quarter, wide = body.shape
    size, half = wide // 2, wide // 4
    rows = jnp.concatenate([body[:, :size], body[:, size:]], axis=0)
    corner, side = rows[:, :half], rows[:, half:]
    turned = corner.T
    row, col = iota((half, half), 0), iota((half, half), 1)
    first = jnp.where(col > row, corner, turned)
    last = jnp.where(col < row, corner, turned)
    whole = jnp.concatenate(
        [jnp.concatenate([first, side], axis=1), jnp.concatenate([side.T, last], axis=1)], axis=0
    )
    return jnp.where(iota((size, size), 0) == iota((size, size), 1), diag[:, :size], whole)


def pack_one(whole):
    size = whole.shape[0]
    half, quarter = size // 2, size // 4
    row, col = iota((half, half), 0), iota((half, half), 1)
    corner = jnp.where(row > col, whole[half:, half:], whole[:half, :half])
    rows = jnp.concatenate([corner, whole[:half, half:]], axis=1)
    body = jnp.concatenate([rows[:quarter], rows[quarter:]], axis=1)
    on = jnp.where(iota((size, size), 0) == iota((size, size), 1), whole, 0.0)
    on = jnp.sum(on, axis=0, keepdims=True)
    return body, jnp.concatenate([on, on], axis=1)


def exchange_kernel(
    nz, nt, entries, table, og, gw, fa, update_o, fresh_o,
    ybuf, gbuf, fbuf, gram, dgram, hess, dhess, pos_v, pos,
    amine, asend, arecv, asum, agot, admine, adsend, adrecv, adsum, adgot,
    hmine, hsend, hrecv, hsum, hgot, hdmine, hdsend, hdrecv, hdsum, hdgot,
    xs, xd, xall, xdall, inn, tin, xin, cin, lsem, ssem, rsem,
):
    refresh, layers, tokens, columns = ybuf.shape
    slots, quarter, wide = gram.shape
    size = wide // 2
    per_layer = columns // size
    chips = slots // 2
    others = chips - 1
    dp = lax.axis_index("dp")
    t = lax.axis_index("tensor")
    core = lax.rem(dp, 2)
    here = lax.div(dp, 2)
    xh = lax.div(here, nz)
    z = lax.rem(here, nz)
    mate = (dp + 1 - 2 * core, t)

    copies = [
        [pltpu.make_async_copy(og.at[i, l], ybuf.at[i, l], lsem.at[l * refresh + i]) for i in range(refresh)]
        for l in range(layers)
    ]
    gcopy = pltpu.make_async_copy(gw, gbuf, lsem.at[layers * refresh])
    fcopy = pltpu.make_async_copy(fa, fbuf, lsem.at[layers * refresh + 1])
    for group in copies:
        for cp in group:
            cp.start()
    gcopy.start()
    fcopy.start()

    sides = [xh * nz, (1 - xh) * nz]
    order, origin = [], []
    for j in range(nz):
        k = nz // 2 + (j + 1) // 2 * (1 - 2 * (j % 2))
        there, back = lax.rem(z + k, nz), lax.rem(z + nz - k, nz)
        order += [sides[1] + there, sides[0] + there]
        origin += [sides[1] + back, sides[0] + back]
    peers = [(q * 2 + core, t) for q in order[:others]]
    tpeers = [(dp, lax.rem(t + k, nt)) for k in range(1, nt)]

    barrier = pltpu.get_barrier_semaphore()
    for peer in peers + tpeers + [mate]:
        pl.semaphore_signal(barrier, inc=1, device_id=peer, device_id_type=MESH)

    def send(n, src, dst, peer):
        return pltpu.make_async_remote_copy(
            src_ref=src, dst_ref=dst, send_sem=ssem.at[n], recv_sem=rsem.at[n],
            device_id=peer, device_id_type=MESH,
        )

    weights = [
        (1.0 - AVERAGE_DECAY) * AVERAGE_DECAY ** (refresh - 1 - i) / entries[0] for i in range(refresh)
    ]
    for l in range(layers):
        for cp in copies[l]:
            cp.wait()
        for p in range(per_layer // 2):
            total = None
            for i in range(refresh):
                y = ybuf[i, l, :, wide * p : wide * (p + 1)]
                part = weights[i] * lax.dot_general(
                    y, y, (((0,), (0,)), ((), ())), preferred_element_type=F32
                )
                total = part if total is None else total + part
            pack_pair(total, gram, dgram, l * per_layer + 2 * p)

    def arrange(body, diag, mine, away, dmine, daway):
        for i in range(chips):
            b = table[2 * order[i] + core]
            mine[i] = body[b]
            dmine[i] = diag[b]
            b = table[2 * order[i] + 1 - core]
            away[i] = body[b].astype(BF16)
            daway[i] = diag[b]

    def reduce_scatter(n, mine, away, recv, total, got, dmine, daway, drecv, dtotal, dgot):
        swap = [send(n, away, recv, mate), send(n + 1, daway, drecv, mate)]
        for cp in swap:
            cp.start()
        for cp in swap:
            cp.wait_recv()
        own = mine[others] + recv[others].astype(F32)
        down = dmine[others] + drecv[others]
        total[...] = (mine[:others] + recv[:others].astype(F32)).astype(BF16)
        dtotal[...] = dmine[:others] + drecv[:others]
        for i in range(others):
            send(n + 2, total.at[i], got.at[i], peers[i]).start()
            send(n + 3, dtotal.at[i], dgot.at[i], peers[i]).start()
        whole = [send(n + 2, total, got, mate), send(n + 3, dtotal, dgot, mate)]
        return own, down, swap, whole

    def collect(own, down, whole, got, dgot):
        for cp in whole:
            cp.wait_recv()
        return own + jnp.sum(got[...].astype(F32), axis=0), down + jnp.sum(dgot[...], axis=0)

    arrange(gram, dgram, amine, asend, admine, adsend)
    pl.semaphore_wait(barrier, others + nt)
    own, down, aswap, awhole = reduce_scatter(
        0, amine, asend, arecv, asum, agot, admine, adsend, adrecv, adsum, adgot
    )

    gcopy.wait()
    for l in range(layers):
        for p in range(per_layer // 2):
            g = gbuf[l, :, wide * p : wide * (p + 1)]
            total = lax.dot_general(g, g, (((0,), (0,)), ((), ())), preferred_element_type=F32)
            pack_pair(total, hess, dhess, l * per_layer + 2 * p)
    arrange(hess, dhess, hmine, hsend, hdmine, hdsend)
    hown, hdown, hswap, hwhole = reduce_scatter(
        4, hmine, hsend, hrecv, hsum, hgot, hdmine, hdsend, hdrecv, hdsum, hdgot
    )
    lane = iota(pos_v.shape, 1)
    place = jnp.zeros(pos_v.shape, jnp.int32)
    for j in range(slots):
        owner = core if j < chips else 1 - core
        place = jnp.where(lane == table[2 * origin[j % chips] + owner], j, place)
    pos_v[...] = place
    pcopy = pltpu.make_async_copy(pos_v, pos, lsem.at[layers * refresh + 2])
    pcopy.start()
    pcopy.wait()
    fcopy.wait()

    body, diag = collect(own, down, awhole, agot, adgot)
    fresh = AVERAGE_DECAY**refresh * fbuf[0] + unpack(body, diag)
    fresh_o[0] = fresh
    on = iota((size, size), 0) == iota((size, size), 1)
    inverse = newton_schulz(fresh + jnp.where(on, DAMPING, 0.0))
    xbody, xdiag = pack_one(inverse)
    xbody, xdiag = xbody.astype(BF16), xdiag.astype(BF16).astype(F32)
    xs[...] = xbody
    xd[...] = xdiag
    xall[others] = xbody
    xdall[others] = xdiag
    for i in range(others):
        send(8, xs, xall.at[i], peers[i]).start()
        send(9, xd, xdall.at[i], peers[i]).start()

    hbody, hdiag = collect(hown, hdown, hwhole, hgot, hdgot)
    lane = iota((quarter, wide), 1)
    row = iota((quarter, wide), 0)
    local = jnp.where(lane < size, lane, lane - size - quarter)
    twice = jnp.where(local == row, 0.0, 2.0)
    once = jnp.where(iota((1, wide), 1) < size, xdiag * hdiag, 0.0)
    partial = jnp.sum(twice * xbody.astype(F32) * hbody, axis=0, keepdims=True) + once
    inn[0] = partial
    for k in range(nt - 1):
        send(10, inn.at[0], tin.at[k], tpeers[k]).start()
    tin_all = pltpu.make_async_remote_copy(
        src_ref=tin, dst_ref=tin, send_sem=ssem.at[10], recv_sem=rsem.at[10],
        device_id=mate, device_id_type=MESH,
    )
    tin_all.wait_recv()
    partial = partial + jnp.sum(tin[...], axis=0)
    inn[1] = partial
    for i in range(others):
        send(11, inn.at[1], xin.at[i], peers[i]).start()

    direct = xall.at[pl.ds(0, others)]
    ddirect = xdall.at[pl.ds(0, others)]
    xwhole = [send(8, direct, direct, mate), send(9, ddirect, ddirect, mate)]
    for cp in xwhole:
        cp.wait_recv()
    near, far = pl.ds(0, chips), pl.ds(chips, chips)
    forward = [
        send(12, xall.at[near], xall.at[far], mate),
        send(13, xdall.at[near], xdall.at[far], mate),
    ]
    for cp in forward:
        cp.start()
    xin_all = send(11, xin, xin, mate)
    xin_all.wait_recv()
    partial = partial + jnp.sum(xin[...], axis=0)
    inn[2] = partial
    ccopy = send(14, inn.at[2], cin, mate)
    ccopy.start()
    for cp in forward:
        cp.wait_recv()
    ccopy.wait_recv()
    inner = jnp.sum(partial + cin[...], axis=1, keepdims=True)
    clip = jnp.minimum(1.0, jnp.sqrt(KL_CLIP * entries[1] / inner))

    half = size // 2
    row, lane = iota((half, size), 0), iota((half, size), 1)

    def apply(b, g):
        q = pos[0, b]
        x = xall[q].astype(F32)
        d = 0.5 * xdall[q][:, :size]
        rows = jnp.concatenate([x[:, :size], x[:, size:]], axis=0)
        top = jnp.where(lane > row, rows, jnp.where(lane == row, d, 0.0))
        moved = jnp.concatenate([rows[:, half:], rows[:, :half]], axis=1)
        low = jnp.where(
            (lane >= half) & (lane - half < row), moved, jnp.where(lane - half == row, d, 0.0)
        )
        v = jnp.concatenate([top, low], axis=0).astype(BF16)
        out = jnp.dot(g, v, preferred_element_type=F32)
        out = out + lax.dot_general(g, v, (((1,), (1,)), ((), ())), preferred_element_type=F32)
        return out.astype(BF16).astype(F32)

    for l in range(layers):
        for p in range(per_layer // 2):
            b = l * per_layer + 2 * p
            g = gbuf[l, :, wide * p : wide * (p + 1)]
            out = jnp.concatenate([apply(b, g[:, :size]), apply(b + 1, g[:, size:])], axis=1)
            update_o[l, :, wide * p : wide * (p + 1)] = (clip * out).astype(BF16)

    for cp in aswap + awhole + hswap + hwhole + forward + [ccopy]:
        cp.wait_send()
    for i in range(others):
        send(8, xs, xall.at[i], peers[i]).wait_send()
        send(9, xd, xdall.at[i], peers[i]).wait_send()
        send(11, inn.at[1], xin.at[i], peers[i]).wait_send()
    for k in range(nt - 1):
        send(10, inn.at[0], tin.at[k], tpeers[k]).wait_send()


def finish_kernel(update, fresh, update_o, fresh_o):
    update_o[...] = update[...]
    fresh_o[...] = fresh[...]


def shards(out_grads, grad_w, factor_avg, owner_table):
    refresh, layers, tokens, columns = out_grads.shape
    _, size, _ = factor_avg.shape
    rows = grad_w.shape[1]
    slots = owner_table.shape[0]
    n_dp = lax.axis_size("dp")
    nt = lax.axis_size("tensor")
    nz = n_dp // 4
    chips = slots // 2
    others = chips - 1
    quarter, wide = size // 4, 2 * size
    entries = (float(tokens * n_dp), float(layers * rows * n_dp * columns * nt))
    hbm = pl.BlockSpec(memory_space=pltpu.HBM)
    vmem = pl.BlockSpec(memory_space=pltpu.VMEM)
    smem = pl.BlockSpec(memory_space=pltpu.SMEM)

    def body(n, dtype):
        return pltpu.VMEM((n, quarter, wide), dtype)

    def line(n):
        return pltpu.VMEM((n, 1, wide), F32)

    buffers = [
        body(chips, F32), body(chips, BF16), body(chips, BF16), body(others, BF16), body(others, BF16),
        line(chips), line(chips), line(chips), line(others), line(others),
    ]
    results = (
        jax.ShapeDtypeStruct(grad_w.shape, BF16),
        jax.ShapeDtypeStruct(factor_avg.shape, F32),
    )
    update, fresh = pl.pallas_call(
        functools.partial(exchange_kernel, nz, nt, entries),
        out_shape=results,
        in_specs=[smem, hbm, hbm, hbm],
        out_specs=(vmem, vmem),
        scratch_shapes=[
            pltpu.VMEM(out_grads.shape, BF16),
            pltpu.VMEM(grad_w.shape, BF16),
            pltpu.VMEM(factor_avg.shape, F32),
            body(slots, F32), line(slots), body(slots, F32), line(slots),
            pltpu.VMEM((8, 128), jnp.int32),
            pltpu.SMEM((8, 128), jnp.int32),
            *buffers,
            *buffers,
            pltpu.VMEM((quarter, wide), BF16),
            pltpu.VMEM((1, wide), F32),
            body(slots, BF16), line(slots),
            line(3), line(nt - 1), line(others), pltpu.VMEM((1, wide), F32),
            pltpu.SemaphoreType.DMA((layers * refresh + 3,)),
            pltpu.SemaphoreType.DMA((15,)),
            pltpu.SemaphoreType.DMA((15,)),
        ],
        compiler_params=pltpu.CompilerParams(
            collective_id=0, has_side_effects=True, vmem_limit_bytes=VMEM_KIB * 1024
        ),
        name="exchange",
    )(owner_table, out_grads, grad_w, factor_avg)
    return pl.pallas_call(
        finish_kernel,
        out_shape=results,
        in_specs=[vmem, vmem],
        out_specs=(vmem, vmem),
        name="finish",
    )(update, fresh)


VMEM_KIB = 63 * 1024 + 640


def solution(mesh):
    placed = (
        P(None, None, "dp", "tensor"),
        P(None, "dp", "tensor"),
        P(("dp", "tensor"), None, None),
        P(),
    )
    return jax.shard_map(
        shards,
        mesh=mesh,
        in_specs=placed,
        out_specs=(P(None, "dp", "tensor"), P(("dp", "tensor"), None, None)),
        check_vma=False,
    )
```

time: 433 us -> 54.4 us (0.13)
  waiting for transfers between devices: 205 us -> 0 us
  blocking collectives: 189 us -> 0 us
  Pallas kernels: 0 us -> 53.6 us
  between operations: 15.7 us -> 0.64 us
  local copies, waits for them, and re-layouts: 11.4 us -> 0 us
  matrix products: 6.38 us -> 0 us
  other arithmetic: 5.8 us -> 0 us
    reduce_scatter x1 -> x0, waiting for transfers between devices: 205 us -> none  [shards(): grams = lax.psum_scatter(summed, 'dp', scatter_dimension=0, tiled=True)]
    psum x1 -> x0, blocking collectives: 101 us -> none  [shards(): inner = lax.psum(local_inner, ('dp', 'tensor'))]
    all_gather x1 -> x0, blocking collectives: 88.1 us -> none  [shards(): lax.all_gather(inverse_half, 'dp', axis=0, tiled=True)]
    pallas_call x0 -> x2, Pallas kernels: none -> 53.6 us  [the longest x1 52 us: shards(): pl.pallas_call(functools.partial(exchange_kernel, nz, nt, entries), out_s...]
    dot_general x20 -> x0, matrix products: 6.38 us -> none  [the longest x3 3.4 us: shards(): jnp.einsum('qtb,qtc->qbc', portion, portion, preferred_element_type=jnp.f...]
    unnamed x9 -> x0, local copies, waits for them, and re-layouts: 5.63 us -> none
    gather x3 -> x0, local copies, waits for them, and re-layouts: 4.35 us -> none  [the longest x1 3.04 us: shards(): picked = split_grads[:, chosen // per_layer, :, chosen % per_layer, :]]
  transfers between devices with their start and end apart: 1 -> 0, of which waited for: 1 -> 0; matrix products, arithmetic and copies ran while one was open for 1% -> 0% of each run, Pallas kernels for 0% -> 0%
where the time goes in v2:
time: 54.4 us; the launch traced here: 54.3 us
  Pallas kernels  53.6 us (99%)
  between operations  0.64 us (1%)
    pallas_call x1, Pallas kernels, shards(): pl.pallas_call(functools.partial(exchange_kernel, nz, nt, entries), out_s...  52 us
    pallas_call x1, Pallas kernels, shards(): pl.pallas_call(finish_kernel, out_shape=results, in_specs=[vmem, vmem], o...  1.68 us

profile of v2, /device:TPU:1, one launch (start us, length us, event | category | flops | bytes accessed | tf_op | source)
XLA Modules:
  0.0 54.3 jit_solution(14962363444114592001)
XLA Ops:
  0.6 52.0 %exchange.1 = (bf16[4,32,1024]{2,1,0:T(8,128)(2,1)}, f32[1,64,64]{2,1,0:T(8,128)}) custom-call(s32[64]{0:T(128)} %table.1, bf16[3,4,128,1024]{3,2,1,0:T(8,128)(2,1)} %og.1, bf16[4,32,1024]{2,1,0:T(8,128)(2,1)} %gw.1, f32[1,64,64]{2,1,0:T(8,128)} %fa.1), custom_call_target="tpu_custom_call" | custom-call | tf_op jit(solution)/shard_map/exchange/pallas_call | solution.py:343
  52.6 1.7 %finish.1 = (bf16[4,32,1024]{2,1,0:T(8,128)(2,1)}, f32[1,64,64]{2,1,0:T(8,128)}) custom-call(bf16[4,32,1024]{2,1,0:T(8,128)(2,1)} %get-tuple-element.4.update, f32[1,64,64]{2,1,0:T(8,128)} %get-tuple-element.5.fresh), custom_call_target="tpu_custom_call" | custom-call | tf_op jit(solution)/shard_map/finish/pallas_call | solution.py:370

commit v3 on v2

--- a/solution.py
+++ b/solution.py
@@ -86,11 +86,11 @@
 
 
 def exchange_kernel(
-    nz, nt, entries, table, og, gw, fa, update_o, fresh_o,
-    ybuf, gbuf, fbuf, gram, dgram, hess, dhess, pos_v, pos,
+    nz, nt, entries, owners, og, gw, fa, update_o, fresh_o,
+    table, ybuf, gbuf, fbuf, gram, dgram, hess, dhess, pos_v, pos,
     amine, asend, arecv, asum, agot, admine, adsend, adrecv, adsum, adgot,
     hmine, hsend, hrecv, hsum, hgot, hdmine, hdsend, hdrecv, hdsum, hdgot,
-    xs, xd, xall, xdall, inn, tin, xin, cin, lsem, ssem, rsem,
+    hleave, hacross, hdacross, xs, xd, xall, xdall, inn, pin, zin, pre, lsem, ssem, rsem,
 ):
     refresh, layers, tokens, columns = ybuf.shape
     slots, quarter, wide = gram.shape
@@ -110,33 +110,52 @@
         [pltpu.make_async_copy(og.at[i, l], ybuf.at[i, l], lsem.at[l * refresh + i]) for i in range(refresh)]
         for l in range(layers)
     ]
+    tcopy = pltpu.make_async_copy(owners, table, lsem.at[layers * refresh + 3])
     gcopy = pltpu.make_async_copy(gw, gbuf, lsem.at[layers * refresh])
     fcopy = pltpu.make_async_copy(fa, fbuf, lsem.at[layers * refresh + 1])
+    sides = [xh * nz, (1 - xh) * nz]
+    steps = [nz // 2 + (j + 1) // 2 * (1 - 2 * (j % 2)) for j in range(nz)]
+    there = [lax.rem(z + k, nz) for k in steps]
+    back = [lax.rem(z + nz - k, nz) for k in steps]
+    order = [sides[1] + q for q in there] + [sides[0] + q for q in there]
+    origin = [sides[1] + q for q in back] + [sides[0] + q for q in back]
+    peers = [(q * 2 + core, t) for q in order[:others]]
+    issue = [i for j in range(nz) for i in (j, nz + j) if i < others]
+    across = peers[nz - 1]
+    zpeers = peers[nz:]
+    plane = []
+    for a in range(2):
+        for c in range(2):
+            for k in range(nt):
+                if a + c + k:
+                    plane.append(
+                        ((sides[a] + z) * 2 + (core if c == 0 else 1 - core), lax.rem(t + k, nt))
+                    )
+    greeted = [peers[i] for i in issue]
+    greeted += [p for n, p in enumerate(plane) if n + 1 not in (nt, 2 * nt)] + [mate]
+
+    barrier = pltpu.get_barrier_semaphore()
+    for peer in greeted:
+        pl.semaphore_signal(barrier, inc=1, device_id=peer, device_id_type=MESH)
+    tcopy.start()
+    gcopy.start()
     for group in copies:
         for cp in group:
             cp.start()
-    gcopy.start()
     fcopy.start()
-
-    sides = [xh * nz, (1 - xh) * nz]
-    order, origin = [], []
-    for j in range(nz):
-        k = nz // 2 + (j + 1) // 2 * (1 - 2 * (j % 2))
-        there, back = lax.rem(z + k, nz), lax.rem(z + nz - k, nz)
-        order += [sides[1] + there, sides[0] + there]
-        origin += [sides[1] + back, sides[0] + back]
-    peers = [(q * 2 + core, t) for q in order[:others]]
-    tpeers = [(dp, lax.rem(t + k, nt)) for k in range(1, nt)]
-
-    barrier = pltpu.get_barrier_semaphore()
-    for peer in peers + tpeers + [mate]:
-        pl.semaphore_signal(barrier, inc=1, device_id=peer, device_id_type=MESH)
 
     def send(n, src, dst, peer):
         return pltpu.make_async_remote_copy(
             src_ref=src, dst_ref=dst, send_sem=ssem.at[n], recv_sem=rsem.at[n],
             device_id=peer, device_id_type=MESH,
         )
+
+    gcopy.wait()
+    for l in range(layers):
+        for p in range(per_layer // 2):
+            g = gbuf[l, :, wide * p : wide * (p + 1)]
+            total = lax.dot_general(g, g, (((0,), (0,)), ((), ())), preferred_element_type=F32)
+            pack_pair(total, hess, dhess, l * per_layer + 2 * p)
 
     weights = [
         (1.0 - AVERAGE_DECAY) * AVERAGE_DECAY ** (refresh - 1 - i) / entries[0] for i in range(refresh)
@@ -163,43 +182,36 @@
             away[i] = body[b].astype(BF16)
             daway[i] = diag[b]
 
-    def reduce_scatter(n, mine, away, recv, total, got, dmine, daway, drecv, dtotal, dgot):
-        swap = [send(n, away, recv, mate), send(n + 1, daway, drecv, mate)]
-        for cp in swap:
-            cp.start()
-        for cp in swap:
-            cp.wait_recv()
-        own = mine[others] + recv[others].astype(F32)
-        down = dmine[others] + drecv[others]
-        total[...] = (mine[:others] + recv[:others].astype(F32)).astype(BF16)
-        dtotal[...] = dmine[:others] + drecv[:others]
-        for i in range(others):
-            send(n + 2, total.at[i], got.at[i], peers[i]).start()
-            send(n + 3, dtotal.at[i], dgot.at[i], peers[i]).start()
-        whole = [send(n + 2, total, got, mate), send(n + 3, dtotal, dgot, mate)]
-        return own, down, swap, whole
-
-    def collect(own, down, whole, got, dgot):
-        for cp in whole:
-            cp.wait_recv()
-        return own + jnp.sum(got[...].astype(F32), axis=0), down + jnp.sum(dgot[...], axis=0)
-
+    tcopy.wait()
     arrange(gram, dgram, amine, asend, admine, adsend)
-    pl.semaphore_wait(barrier, others + nt)
-    own, down, aswap, awhole = reduce_scatter(
-        0, amine, asend, arecv, asum, agot, admine, adsend, adrecv, adsum, adgot
-    )
-
-    gcopy.wait()
-    for l in range(layers):
-        for p in range(per_layer // 2):
-            g = gbuf[l, :, wide * p : wide * (p + 1)]
-            total = lax.dot_general(g, g, (((0,), (0,)), ((), ())), preferred_element_type=F32)
-            pack_pair(total, hess, dhess, l * per_layer + 2 * p)
     arrange(hess, dhess, hmine, hsend, hdmine, hdsend)
-    hown, hdown, hswap, hwhole = reduce_scatter(
-        4, hmine, hsend, hrecv, hsum, hgot, hdmine, hdsend, hdrecv, hdsum, hdgot
-    )
+    pl.semaphore_wait(barrier, len(greeted))
+
+    aswap = [send(0, asend, arecv, mate), send(1, adsend, adrecv, mate)]
+    hswap = [send(2, hsend, hrecv, mate), send(3, hdsend, hdrecv, mate)]
+    for cp in aswap + hswap:
+        cp.start()
+
+    for cp in aswap:
+        cp.wait_recv()
+    asum[...] = (amine[:others] + arecv[:others].astype(F32)).astype(BF16)
+    adsum[...] = admine[:others] + adrecv[:others]
+    for i in issue:
+        send(4, asum.at[i], agot.at[i], peers[i]).start()
+        send(5, adsum.at[i], adgot.at[i], peers[i]).start()
+
+    for cp in hswap:
+        cp.wait_recv()
+    hmine[...] = hmine[...] + hrecv[...].astype(F32)
+    hdmine[...] = hdmine[...] + hdrecv[...]
+    hleave[...] = hmine[:nz].astype(BF16)
+    xswap = [
+        send(6, hleave, hacross, across),
+        send(7, hdmine.at[pl.ds(0, nz)], hdacross, across),
+    ]
+    for cp in xswap:
+        cp.start()
+
     lane = iota(pos_v.shape, 1)
     place = jnp.zeros(pos_v.shape, jnp.int32)
     for j in range(slots):
@@ -208,10 +220,23 @@
     pos_v[...] = place
     pcopy = pltpu.make_async_copy(pos_v, pos, lsem.at[layers * refresh + 2])
     pcopy.start()
+    for cp in xswap:
+        cp.wait_recv()
+    hmine[nz:] = hmine[nz:] + hacross[...].astype(F32)
+    hdmine[nz:] = hdmine[nz:] + hdacross[...]
+    hsum[...] = hmine[nz:others].astype(BF16)
+    hdsum[...] = hdmine[nz:others]
+    for i in range(nz - 1):
+        send(8, hsum.at[i], hgot.at[i], zpeers[i]).start()
+        send(9, hdsum.at[i], hdgot.at[i], zpeers[i]).start()
     pcopy.wait()
     fcopy.wait()
 
-    body, diag = collect(own, down, awhole, agot, adgot)
+    awhole = [send(4, asum, agot, mate), send(5, adsum, adgot, mate)]
+    for cp in awhole:
+        cp.wait_recv()
+    body = amine[others] + arecv[others].astype(F32) + jnp.sum(agot[...].astype(F32), axis=0)
+    diag = admine[others] + adrecv[others] + jnp.sum(adgot[...], axis=0)
     fresh = AVERAGE_DECAY**refresh * fbuf[0] + unpack(body, diag)
     fresh_o[0] = fresh
     on = iota((size, size), 0) == iota((size, size), 1)
@@ -222,11 +247,15 @@
     xd[...] = xdiag
     xall[others] = xbody
     xdall[others] = xdiag
-    for i in range(others):
-        send(8, xs, xall.at[i], peers[i]).start()
-        send(9, xd, xdall.at[i], peers[i]).start()
-
-    hbody, hdiag = collect(hown, hdown, hwhole, hgot, hdgot)
+    for i in issue:
+        send(10, xs, xall.at[i], peers[i]).start()
+        send(11, xd, xdall.at[i], peers[i]).start()
+
+    hwhole = [send(8, hsum, hgot, mate), send(9, hdsum, hdgot, mate)]
+    for cp in hwhole:
+        cp.wait_recv()
+    hbody = hmine[others] + jnp.sum(hgot[...].astype(F32), axis=0)
+    hdiag = hdmine[others] + jnp.sum(hdgot[...], axis=0)
     lane = iota((quarter, wide), 1)
     row = iota((quarter, wide), 0)
     local = jnp.where(lane < size, lane, lane - size - quarter)
@@ -234,41 +263,28 @@
     once = jnp.where(iota((1, wide), 1) < size, xdiag * hdiag, 0.0)
     partial = jnp.sum(twice * xbody.astype(F32) * hbody, axis=0, keepdims=True) + once
     inn[0] = partial
-    for k in range(nt - 1):
-        send(10, inn.at[0], tin.at[k], tpeers[k]).start()
-    tin_all = pltpu.make_async_remote_copy(
-        src_ref=tin, dst_ref=tin, send_sem=ssem.at[10], recv_sem=rsem.at[10],
-        device_id=mate, device_id_type=MESH,
-    )
-    tin_all.wait_recv()
-    partial = partial + jnp.sum(tin[...], axis=0)
+    for n, peer in enumerate(plane):
+        send(12, inn.at[0], pin.at[n], peer).start()
+    pin_all = send(12, pin, pin, mate)
+    pin_all.wait_recv()
+    partial = partial + jnp.sum(pin[...], axis=0)
     inn[1] = partial
-    for i in range(others):
-        send(11, inn.at[1], xin.at[i], peers[i]).start()
-
-    direct = xall.at[pl.ds(0, others)]
-    ddirect = xdall.at[pl.ds(0, others)]
-    xwhole = [send(8, direct, direct, mate), send(9, ddirect, ddirect, mate)]
+    for i in range(nz - 1):
+        send(13, inn.at[1], zin.at[i], zpeers[i]).start()
+
+    direct, ddirect = xall.at[pl.ds(0, others)], xdall.at[pl.ds(0, others)]
+    xwhole = [send(10, direct, direct, mate), send(11, ddirect, ddirect, mate)]
     for cp in xwhole:
         cp.wait_recv()
     near, far = pl.ds(0, chips), pl.ds(chips, chips)
     forward = [
-        send(12, xall.at[near], xall.at[far], mate),
-        send(13, xdall.at[near], xdall.at[far], mate),
+        send(14, xall.at[near], xall.at[far], mate),
+        send(15, xdall.at[near], xdall.at[far], mate),
     ]
     for cp in forward:
         cp.start()
-    xin_all = send(11, xin, xin, mate)
-    xin_all.wait_recv()
-    partial = partial + jnp.sum(xin[...], axis=0)
-    inn[2] = partial
-    ccopy = send(14, inn.at[2], cin, mate)
-    ccopy.start()
     for cp in forward:
         cp.wait_recv()
-    ccopy.wait_recv()
-    inner = jnp.sum(partial + cin[...], axis=1, keepdims=True)
-    clip = jnp.minimum(1.0, jnp.sqrt(KL_CLIP * entries[1] / inner))
 
     half = size // 2
     row, lane = iota((half, size), 0), iota((half, size), 1)
@@ -286,28 +302,37 @@
         v = jnp.concatenate([top, low], axis=0).astype(BF16)
         out = jnp.dot(g, v, preferred_element_type=F32)
         out = out + lax.dot_general(g, v, (((1,), (1,)), ((), ())), preferred_element_type=F32)
-        return out.astype(BF16).astype(F32)
+        return out.astype(BF16)
 
     for l in range(layers):
         for p in range(per_layer // 2):
             b = l * per_layer + 2 * p
             g = gbuf[l, :, wide * p : wide * (p + 1)]
             out = jnp.concatenate([apply(b, g[:, :size]), apply(b + 1, g[:, size:])], axis=1)
-            update_o[l, :, wide * p : wide * (p + 1)] = (clip * out).astype(BF16)
-
-    for cp in aswap + awhole + hswap + hwhole + forward + [ccopy]:
+            pre[l, :, wide * p : wide * (p + 1)] = out
+
+    for cp in aswap + awhole + hswap + xswap + hwhole + xwhole + forward + [pin_all]:
         cp.wait_send()
-    for i in range(others):
-        send(8, xs, xall.at[i], peers[i]).wait_send()
-        send(9, xd, xdall.at[i], peers[i]).wait_send()
-        send(11, inn.at[1], xin.at[i], peers[i]).wait_send()
-    for k in range(nt - 1):
-        send(10, inn.at[0], tin.at[k], tpeers[k]).wait_send()
-
-
-def finish_kernel(update, fresh, update_o, fresh_o):
-    update_o[...] = update[...]
-    fresh_o[...] = fresh[...]
+    zin_all = send(13, zin, zin, mate)
+    zin_all.wait_recv()
+    partial = partial + jnp.sum(zin[...], axis=0)
+    inner = jnp.sum(partial, axis=1, keepdims=True)
+    clip = jnp.minimum(1.0, jnp.sqrt(KL_CLIP * entries[1] / inner))
+    for l in range(layers):
+        update_o[l] = (clip * pre[l].astype(F32)).astype(BF16)
+
+    zin_all.wait_send()
+
+
+def finish_kernel(update, fresh, update_o, fresh_o, sems):
+    copies = [
+        pltpu.make_async_copy(update, update_o, sems.at[0]),
+        pltpu.make_async_copy(fresh, fresh_o, sems.at[1]),
+    ]
+    for cp in copies:
+        cp.start()
+    for cp in copies:
+        cp.wait()
 
 
 def shards(out_grads, grad_w, factor_avg, owner_table):
@@ -324,7 +349,6 @@
     entries = (float(tokens * n_dp), float(layers * rows * n_dp * columns * nt))
     hbm = pl.BlockSpec(memory_space=pltpu.HBM)
     vmem = pl.BlockSpec(memory_space=pltpu.VMEM)
-    smem = pl.BlockSpec(memory_space=pltpu.SMEM)
 
     def body(n, dtype):
         return pltpu.VMEM((n, quarter, wide), dtype)
@@ -332,46 +356,53 @@
     def line(n):
         return pltpu.VMEM((n, 1, wide), F32)
 
-    buffers = [
-        body(chips, F32), body(chips, BF16), body(chips, BF16), body(others, BF16), body(others, BF16),
-        line(chips), line(chips), line(chips), line(others), line(others),
-    ]
-    results = (
-        jax.ShapeDtypeStruct(grad_w.shape, BF16),
-        jax.ShapeDtypeStruct(factor_avg.shape, F32),
-    )
+    def buffers(n):
+        return [
+            body(chips, F32), body(chips, BF16), body(chips, BF16), body(n, BF16), body(n, BF16),
+            line(chips), line(chips), line(chips), line(n), line(n),
+        ]
+
     update, fresh = pl.pallas_call(
         functools.partial(exchange_kernel, nz, nt, entries),
-        out_shape=results,
-        in_specs=[smem, hbm, hbm, hbm],
+        out_shape=(pltpu.VMEM(grad_w.shape, BF16), pltpu.VMEM(factor_avg.shape, F32)),
+        in_specs=[hbm, hbm, hbm, hbm],
         out_specs=(vmem, vmem),
         scratch_shapes=[
+            pltpu.SMEM(owner_table.shape, jnp.int32),
             pltpu.VMEM(out_grads.shape, BF16),
             pltpu.VMEM(grad_w.shape, BF16),
             pltpu.VMEM(factor_avg.shape, F32),
             body(slots, F32), line(slots), body(slots, F32), line(slots),
             pltpu.VMEM((8, 128), jnp.int32),
             pltpu.SMEM((8, 128), jnp.int32),
-            *buffers,
-            *buffers,
+            *buffers(others),
+            *buffers(nz - 1),
+            body(nz, BF16), body(nz, BF16), line(nz),
             pltpu.VMEM((quarter, wide), BF16),
             pltpu.VMEM((1, wide), F32),
             body(slots, BF16), line(slots),
-            line(3), line(nt - 1), line(others), pltpu.VMEM((1, wide), F32),
-            pltpu.SemaphoreType.DMA((layers * refresh + 3,)),
-            pltpu.SemaphoreType.DMA((15,)),
-            pltpu.SemaphoreType.DMA((15,)),
+            line(2), line(4 * nt - 1), line(nz - 1),
+            pltpu.VMEM(grad_w.shape, BF16),
+            pltpu.SemaphoreType.DMA((layers * refresh + 4,)),
+            pltpu.SemaphoreType.DMA((16,)),
+            pltpu.SemaphoreType.DMA((16,)),
         ],
         compiler_params=pltpu.CompilerParams(
             collective_id=0, has_side_effects=True, vmem_limit_bytes=VMEM_KIB * 1024
         ),
         name="exchange",
     )(owner_table, out_grads, grad_w, factor_avg)
+    update = pltpu.with_memory_space_constraint(update, pltpu.VMEM)
+    fresh = pltpu.with_memory_space_constraint(fresh, pltpu.VMEM)
     return pl.pallas_call(
         finish_kernel,
-        out_shape=results,
-        in_specs=[vmem, vmem],
-        out_specs=(vmem, vmem),
+        out_shape=(
+            jax.ShapeDtypeStruct(grad_w.shape, BF16),
+            jax.ShapeDtypeStruct(factor_avg.shape, F32),
+        ),
+        in_specs=[pl.BlockSpec(memory_space=pl.ANY)] * 2,
+        out_specs=[pl.BlockSpec(memory_space=pl.ANY)] * 2,
+        scratch_shapes=[pltpu.SemaphoreType.DMA((2,))],
         name="finish",
     )(update, fresh)
 

time: 54.4 us -> 46.1 us (0.85)
  Pallas kernels: 53.6 us -> 45.3 us
    pallas_call x1, Pallas kernels: 52 us -> 44.6 us  [shards(): pl.pallas_call(functools.partial(exchange_kernel, nz, nt, entries), out_s...]
    pallas_call x1, Pallas kernels: 1.68 us -> 0.72 us  [shards(): pl.pallas_call(finish_kernel, out_shape=(jax.ShapeDtypeStruct(grad_w.shap...]
where the time goes in v3:
time: 46.1 us; the launch traced here: 46 us
  Pallas kernels  45.3 us (98%)
  between operations  0.64 us (1%)
    pallas_call x1, Pallas kernels, shards(): pl.pallas_call(functools.partial(exchange_kernel, nz, nt, entries), out_s...  44.6 us

profile of v3, /device:TPU:1, one launch (start us, length us, event | category | flops | bytes accessed | tf_op | source)
XLA Modules:
  0.0 46.0 jit_solution(4070018482043924449)
XLA Ops:
  0.6 44.6 %exchange.1 = (bf16[4,32,1024]{2,1,0:T(8,128)(2,1)S(1)}, f32[1,64,64]{2,1,0:T(8,128)S(1)}) custom-call(s32[64]{0:T(128)} %owners.1, bf16[3,4,128,1024]{3,2,1,0:T(8,128)(2,1)} %og.1, bf16[4,32,1024]{2,1,0:T(8,128)(2,1)} %gw.1, f32[1,64,64]{2,1,0:T(8,128)} %fa.1), custom_call_target="tpu_custom_call" | custom-call | tf_op jit(solution)/shard_map/exchange/pallas_call | solution.py:365
  45.3 0.7 %finish.1 = (bf16[4,32,1024]{2,1,0:T(8,128)(2,1)}, f32[1,64,64]{2,1,0:T(8,128)}) custom-call(bf16[4,32,1024]{2,1,0:T(8,128)(2,1)S(1)} %get-tuple-element.4.update, f32[1,64,64]{2,1,0:T(8,128)S(1)} %get-tuple-element.5.fresh), custom_call_target="tpu_custom_call" | custom-call | tf_op jit(solution)/shard_map/finish/pallas_call | solution.py:397

commit v4 on v3

--- a/solution.py
+++ b/solution.py
@@ -88,9 +88,8 @@
 def exchange_kernel(
     nz, nt, entries, owners, og, gw, fa, update_o, fresh_o,
     table, ybuf, gbuf, fbuf, gram, dgram, hess, dhess, pos_v, pos,
-    amine, asend, arecv, asum, agot, admine, adsend, adrecv, adsum, adgot,
-    hmine, hsend, hrecv, hsum, hgot, hdmine, hdsend, hdrecv, hdsum, hdgot,
-    hleave, hacross, hdacross, xs, xd, xall, xdall, inn, pin, zin, pre, lsem, ssem, rsem,
+    amine, asend, arecv, asum, agot, dmine, dsend, drecv, dsum, dgot,
+    hmine, hsend, hrecv, hsum, hgot, hleave, hacross, xs, xd, xall, xdall, inn, pin, zin, pre, lsem, ssem, rsem,
 ):
     refresh, layers, tokens, columns = ybuf.shape
     slots, quarter, wide = gram.shape
@@ -173,42 +172,37 @@
                 total = part if total is None else total + part
             pack_pair(total, gram, dgram, l * per_layer + 2 * p)
 
-    def arrange(body, diag, mine, away, dmine, daway):
-        for i in range(chips):
-            b = table[2 * order[i] + core]
-            mine[i] = body[b]
-            dmine[i] = diag[b]
-            b = table[2 * order[i] + 1 - core]
-            away[i] = body[b].astype(BF16)
-            daway[i] = diag[b]
-
     tcopy.wait()
-    arrange(gram, dgram, amine, asend, admine, adsend)
-    arrange(hess, dhess, hmine, hsend, hdmine, hdsend)
+    left = iota((1, wide), 1) < size
+    for i in range(chips):
+        b = table[2 * order[i] + core]
+        amine[i] = gram[b]
+        hmine[i] = hess[b]
+        dmine[i] = jnp.where(left, dgram[b], dhess[b])
+        b = table[2 * order[i] + 1 - core]
+        asend[i] = gram[b].astype(BF16)
+        hsend[i] = hess[b].astype(BF16)
+        dsend[i] = jnp.where(left, dgram[b], dhess[b])
     pl.semaphore_wait(barrier, len(greeted))
 
-    aswap = [send(0, asend, arecv, mate), send(1, adsend, adrecv, mate)]
-    hswap = [send(2, hsend, hrecv, mate), send(3, hdsend, hdrecv, mate)]
+    aswap = [send(0, asend, arecv, mate), send(1, dsend, drecv, mate)]
+    hswap = [send(2, hsend, hrecv, mate)]
     for cp in aswap + hswap:
         cp.start()
 
     for cp in aswap:
         cp.wait_recv()
     asum[...] = (amine[:others] + arecv[:others].astype(F32)).astype(BF16)
-    adsum[...] = admine[:others] + adrecv[:others]
+    dsum[...] = dmine[:others] + drecv[:others]
     for i in issue:
         send(4, asum.at[i], agot.at[i], peers[i]).start()
-        send(5, adsum.at[i], adgot.at[i], peers[i]).start()
+        send(5, dsum.at[i], dgot.at[i], peers[i]).start()
 
     for cp in hswap:
         cp.wait_recv()
     hmine[...] = hmine[...] + hrecv[...].astype(F32)
-    hdmine[...] = hdmine[...] + hdrecv[...]
     hleave[...] = hmine[:nz].astype(BF16)
-    xswap = [
-        send(6, hleave, hacross, across),
-        send(7, hdmine.at[pl.ds(0, nz)], hdacross, across),
-    ]
+    xswap = [send(6, hleave, hacross, across)]
     for cp in xswap:
         cp.start()
 
@@ -223,20 +217,17 @@
     for cp in xswap:
         cp.wait_recv()
     hmine[nz:] = hmine[nz:] + hacross[...].astype(F32)
-    hdmine[nz:] = hdmine[nz:] + hdacross[...]
     hsum[...] = hmine[nz:others].astype(BF16)
-    hdsum[...] = hdmine[nz:others]
     for i in range(nz - 1):
         send(8, hsum.at[i], hgot.at[i], zpeers[i]).start()
-        send(9, hdsum.at[i], hdgot.at[i], zpeers[i]).start()
     pcopy.wait()
     fcopy.wait()
 
-    awhole = [send(4, asum, agot, mate), send(5, adsum, adgot, mate)]
+    awhole = [send(4, asum, agot, mate), send(5, dsum, dgot, mate)]
     for cp in awhole:
         cp.wait_recv()
     body = amine[others] + arecv[others].astype(F32) + jnp.sum(agot[...].astype(F32), axis=0)
-    diag = admine[others] + adrecv[others] + jnp.sum(adgot[...], axis=0)
+    diag = dmine[others] + drecv[others] + jnp.sum(dgot[...], axis=0)
     fresh = AVERAGE_DECAY**refresh * fbuf[0] + unpack(body, diag)
     fresh_o[0] = fresh
     on = iota((size, size), 0) == iota((size, size), 1)
@@ -251,16 +242,15 @@
         send(10, xs, xall.at[i], peers[i]).start()
         send(11, xd, xdall.at[i], peers[i]).start()
 
-    hwhole = [send(8, hsum, hgot, mate), send(9, hdsum, hdgot, mate)]
+    hwhole = [send(8, hsum, hgot, mate)]
     for cp in hwhole:
         cp.wait_recv()
     hbody = hmine[others] + jnp.sum(hgot[...].astype(F32), axis=0)
-    hdiag = hdmine[others] + jnp.sum(hdgot[...], axis=0)
     lane = iota((quarter, wide), 1)
     row = iota((quarter, wide), 0)
     local = jnp.where(lane < size, lane, lane - size - quarter)
     twice = jnp.where(local == row, 0.0, 2.0)
-    once = jnp.where(iota((1, wide), 1) < size, xdiag * hdiag, 0.0)
+    once = jnp.where(left, 0.0, xdiag * diag)
     partial = jnp.sum(twice * xbody.astype(F32) * hbody, axis=0, keepdims=True) + once
     inn[0] = partial
     for n, peer in enumerate(plane):
@@ -357,10 +347,7 @@
         return pltpu.VMEM((n, 1, wide), F32)
 
     def buffers(n):
-        return [
-            body(chips, F32), body(chips, BF16), body(chips, BF16), body(n, BF16), body(n, BF16),
-            line(chips), line(chips), line(chips), line(n), line(n),
-        ]
+        return [body(chips, F32), body(chips, BF16), body(chips, BF16), body(n, BF16), body(n, BF16)]
 
     update, fresh = pl.pallas_call(
         functools.partial(exchange_kernel, nz, nt, entries),
@@ -376,8 +363,9 @@
             pltpu.VMEM((8, 128), jnp.int32),
             pltpu.SMEM((8, 128), jnp.int32),
             *buffers(others),
+            line(chips), line(chips), line(chips), line(others), line(others),
             *buffers(nz - 1),
-            body(nz, BF16), body(nz, BF16), line(nz),
+            body(nz, BF16), body(nz, BF16),
             pltpu.VMEM((quarter, wide), BF16),
             pltpu.VMEM((1, wide), F32),
             body(slots, BF16), line(slots),

time: 46.1 us -> 45.8 us (level)
  no operation moved by 1% of the time
where the time goes in v4:
time: 45.8 us; the launch traced here: 45.7 us
  Pallas kernels  45 us (98%)
  between operations  0.64 us (1%)
    pallas_call x1, Pallas kernels, shards(): pl.pallas_call(functools.partial(exchange_kernel, nz, nt, entries), out_s...  44.3 us

profile of v4, /device:TPU:1, one launch (start us, length us, event | category | flops | bytes accessed | tf_op | source)
XLA Modules:
  0.0 45.7 jit_solution(2588304958853686390)
XLA Ops:
  0.6 44.3 %exchange.1 = (bf16[4,32,1024]{2,1,0:T(8,128)(2,1)S(1)}, f32[1,64,64]{2,1,0:T(8,128)S(1)}) custom-call(s32[64]{0:T(128)} %owners.1, bf16[3,4,128,1024]{3,2,1,0:T(8,128)(2,1)} %og.1, bf16[4,32,1024]{2,1,0:T(8,128)(2,1)} %gw.1, f32[1,64,64]{2,1,0:T(8,128)} %fa.1), custom_call_target="tpu_custom_call" | custom-call | tf_op jit(solution)/shard_map/exchange/pallas_call | solution.py:352
  45.0 0.7 %finish.1 = (bf16[4,32,1024]{2,1,0:T(8,128)(2,1)}, f32[1,64,64]{2,1,0:T(8,128)}) custom-call(bf16[4,32,1024]{2,1,0:T(8,128)(2,1)S(1)} %get-tuple-element.4.update, f32[1,64,64]{2,1,0:T(8,128)S(1)} %get-tuple-element.5.fresh), custom_call_target="tpu_custom_call" | custom-call | tf_op jit(solution)/shard_map/finish/pallas_call | solution.py:385
